TPU v7x, 32 devices: a whole 2x2x4 slice. The times are simulated.
32 devices in a mesh: groups: 2 (over y), seq: 4 (over z), mp: 2 (over x), batch: 2 (over core).
Axes of the slice: x: 2, y: 2, z: 4, core: 2. Of those that a mesh axis runs over, the one named last changes fastest.
Arguments:
- hidden: bfloat16 [4, 1024, 2048], P(('groups', 'batch'), 'seq', 'mp'), parts along dimension 0, may hold values from -6 to 6
- segment_ids: int32 [4, 1024], P(('groups', 'batch'), 'seq'), parts along dimension 0, may hold values from 0 to 3, never falling along the last dimension, each value on 1 to 512 neighbouring positions
- norm_gain: float32 [2048], replicated, may hold values from 0.1 to 1.9
- w_gate: bfloat16 [2048, 2048], P('seq', 'mp'), may hold values from -0.125 to 0.125
- w_value: bfloat16 [2048, 2048], P('seq', 'mp'), may hold values from -0.125 to 0.125
- w_in_out: bfloat16 [2048, 256], P('seq', 'mp'), may hold values from -0.125 to 0.125
- w_step: bfloat16 [2048, 32], P('seq', 'mp'), may hold values from -0.125 to 0.125
- step_bias: float32 [32], P('mp'), may hold values from -3 to -1
- decay_rate: float32 [32], P('mp'), may hold values from 0 to 1, as said below
- skip_gain: float32 [32], P('mp'), may hold values from 0.5 to 1.5
- conv_value: bfloat16 [4, 2048], P(None, 'mp'), may hold values from -3 to 3
- conv_in_out: bfloat16 [4, 256], P(None, 'mp'), may hold values from -3 to 3
- w_out: bfloat16 [2048, 2048], P('mp', 'seq'), may hold values from -0.125 to 0.125
Outputs:
- mixed_out: bfloat16 [4, 1024, 2048], P(('groups', 'batch'), 'seq', 'mp'), parts along dimension 0
There are 2 independent parts, one for each index of `groups`. A program takes and returns all parts, laid end to end along the dimension named above; an argument that names none is the same for every part. Nothing has to cross between parts.
Inputs may be any that keep to these rules, and one draw needn't show every extreme that they name: `decay_rate`: each head's rate is positive and at most 0.15.
All inputs are finite; a program needn't handle non-finite values.
Results may differ from a plain program's by a relative error of at most 0.0076.
Values may be sent and summed in bfloat16 or wider, within the bound.
A program may use at most 64 MiB of HBM per device.

v0:
```python
import jax
import jax.numpy as jnp
from jax import lax
from jax.sharding import PartitionSpec as P

SPAN = 256
GROUP_HEADS = 8


def with_halo(block, sides, width):
    for axis, dim in sides:
        count = lax.axis_size(axis)
        forward = [(i, i + 1) for i in range(count - 1)]
        backward = [(target, source) for source, target in forward]
        low = lax.ppermute(
            lax.slice_in_dim(block, block.shape[dim] - width, None, axis=dim), axis, forward
        )
        high = lax.ppermute(lax.slice_in_dim(block, 0, width, axis=dim), axis, backward)
        block = jnp.concatenate([low, block, high], axis=dim)
    return block


def passed_along(value, axis, by):
    size = lax.axis_size(axis)
    pairs = [(i, i + by) for i in range(size) if 0 <= i + by < size]
    return lax.ppermute(value, axis, pairs)


def entering(value, axis, combine, identity, reverse):
    size, index = (lax.axis_size(axis), lax.axis_index(axis))
    everything = jax.tree.map(
        lambda part, kind: lax.all_gather(part.astype(kind), axis),
        value,
        (jnp.bfloat16, jnp.bfloat16),
    )
    start = jax.tree.map(
        lambda part, zero: jnp.broadcast_to(jnp.asarray(zero, part.dtype), part.shape),
        value,
        identity,
    )

    def lap(k, before):
        at = size - 1 - k if reverse else k
        reached = at > index if reverse else at < index
        new = combine(
            before, jax.tree.map(lambda part, own: part[at].astype(own.dtype), everything, value)
        )
        return jax.tree.map(lambda a, b: jnp.where(reached, a, b), new, before)

    return lax.fori_loop(0, size, lap, start)


def span_terms(values, input_maps, output_maps, log_decay, step_size, segment, segment_before):
    span_rows = values.shape[0]
    cumulative = jnp.cumsum(log_decay, axis=0)
    scores = jnp.dot(output_maps, input_maps.T, preferred_element_type=jnp.float32)
    row_index = lax.broadcasted_iota(jnp.int32, (span_rows, span_rows), 0)
    col_index = lax.broadcasted_iota(jnp.int32, (span_rows, span_rows), 1)
    allowed = (segment[:, None] == segment[None, :]) & (col_index <= row_index)
    cum_heads = cumulative.T
    spread = cum_heads[:, :, None] - cum_heads[:, None, :]
    weights = jnp.where(allowed[None], jnp.exp(jnp.where(allowed[None], spread, 0.0)), 0.0)
    mixing = (scores[None] * weights * step_size.T[:, None, :]).astype(jnp.bfloat16)
    intra_part = jnp.einsum("hij,jhp->ihp", mixing, values, preferred_element_type=jnp.float32)
    final_cum = cumulative[-1]
    same_end = (segment == segment[-1]).astype(jnp.float32)
    to_end = jnp.exp(final_cum[None] - cumulative) * step_size * same_end[:, None]
    weighted = (values.astype(jnp.float32) * to_end[:, :, None]).astype(jnp.bfloat16)
    span_state = jnp.einsum("jhp,jn->hpn", weighted, input_maps, preferred_element_type=jnp.float32)
    inflow = jnp.exp(cumulative) * (segment == segment_before).astype(jnp.float32)[:, None]
    passing = jnp.exp(final_cum) * (segment[-1] == segment_before).astype(jnp.float32)
    return (intra_part, span_state, inflow, passing)


def causal_conv(series, prior_rows, kernel):
    length_rows = series.shape[1]
    padded = jnp.concatenate([prior_rows, series], 1).astype(jnp.float32)
    summed = jnp.zeros(series.shape, jnp.float32)
    for tap_index in range(kernel.shape[0]):
        summed = (
            summed
            + kernel[tap_index].astype(jnp.float32) * padded[:, tap_index : tap_index + length_rows]
        )
    return jax.nn.silu(summed).astype(jnp.bfloat16)


def normalize(block_rows):
    widened = block_rows.astype(jnp.float32)
    return widened * lax.rsqrt(jnp.mean(widened * widened, axis=1, keepdims=True) + 1e-05)


def combine(earlier_part, later_part):
    return (
        earlier_part[0] * later_part[0],
        later_part[0][..., None, None] * earlier_part[1] + later_part[1],
    )


def compose(carried, inputs_pair):
    state_now, decay_now = carried
    span_state, span_pass = inputs_pair
    return (
        (span_pass[..., None, None] * state_now + span_state, decay_now * span_pass),
        (state_now, decay_now),
    )


def body(
    hidden,
    segment_ids,
    norm_gain,
    w_gate,
    w_value,
    w_in_out,
    w_step,
    step_bias,
    decay_rate,
    skip_gain,
    conv_value,
    conv_in_out,
    w_out,
):
    rows_local = hidden[0]
    segment = segment_ids[0]
    tok_count = rows_local.shape[0]
    extended = with_halo(segment, (("seq", 0),), 1)
    forward_full = lax.all_gather(rows_local, "mp", axis=1, tiled=True)
    reverse_full = forward_full[::-1]
    reverse_edges = extended[::-1]
    forward_in = (normalize(forward_full) * norm_gain).astype(jnp.bfloat16)
    reverse_in = (normalize(reverse_full)[:, ::-1] * norm_gain).astype(jnp.bfloat16)
    both_in = jnp.concatenate([forward_in, reverse_in], 0)
    pieces = (
        lax.all_gather(w_gate, "seq", axis=0, tiled=True),
        lax.all_gather(w_value, "seq", axis=0, tiled=True),
        lax.all_gather(w_in_out, "seq", axis=0, tiled=True),
        lax.all_gather(w_step, "seq", axis=0, tiled=True),
    )
    gate_sum, value_sum, inout_sum, step_sum = tuple(
        (jnp.dot(both_in, weight, preferred_element_type=jnp.float32) for weight in pieces)
    )
    gate_all = gate_sum.astype(jnp.bfloat16).reshape(2, tok_count, -1)
    value_pre = value_sum.astype(jnp.bfloat16).reshape(2, tok_count, -1)
    inout_pre = inout_sum.astype(jnp.bfloat16).reshape(2, tok_count, -1)
    reach_rows = conv_value.shape[0] - 1
    value_tail = value_pre[:, tok_count - reach_rows :]
    inout_tail = inout_pre[:, tok_count - reach_rows :]
    forward_prior = passed_along((value_tail[0], inout_tail[0]), "seq", 1)
    reverse_prior = passed_along((value_tail[1], inout_tail[1]), "seq", -1)
    value_prior = jnp.stack([forward_prior[0], reverse_prior[0]])
    inout_prior = jnp.stack([forward_prior[1], reverse_prior[1]])
    values_conv = causal_conv(value_pre, value_prior, conv_value)
    inout_conv = causal_conv(inout_pre, inout_prior, conv_in_out)
    inout_full = lax.all_gather(inout_conv, "mp", axis=2, tiled=True)
    state_width = inout_full.shape[2] // 2
    step_size = jax.nn.softplus(step_sum.reshape(2, tok_count, -1) + step_bias)
    log_decay = -step_size * decay_rate
    heads_local = step_size.shape[2]
    head_width = values_conv.shape[2] // heads_local
    count_spans = tok_count // SPAN
    segments_pair = jnp.stack([extended[1:-1], reverse_edges[1:-1]]).reshape(2, count_spans, SPAN)
    priors_pair = jnp.stack([extended[0], reverse_edges[0]])
    before_pair = jnp.concatenate([priors_pair[:, None], segments_pair[:, :-1, -1]], 1)
    span_values = values_conv.reshape(2, count_spans, SPAN, heads_local, head_width)
    span_inputs = inout_full[..., :state_width].reshape(2, count_spans, SPAN, state_width)
    span_outputs = inout_full[..., state_width:].reshape(2, count_spans, SPAN, state_width)
    span_logs = log_decay.reshape(2, count_spans, SPAN, heads_local)
    span_steps = step_size.reshape(2, count_spans, SPAN, heads_local)
    intra_part, states, inflow, passing = jax.vmap(jax.vmap(span_terms))(
        span_values, span_inputs, span_outputs, span_logs, span_steps, segments_pair, before_pair
    )
    start_pair = (
        jnp.zeros(states.shape[:1] + states.shape[2:], jnp.float32),
        jnp.ones((2, heads_local), jnp.float32),
    )
    summary_pair, before_parts = lax.scan(
        compose, start_pair, (jnp.moveaxis(states, 1, 0), jnp.moveaxis(passing, 1, 0))
    )
    summary_state, summary_decay = summary_pair
    before_states, before_decay = before_parts
    identity = (jnp.ones_like(summary_decay[0]), jnp.zeros_like(summary_state[0]))
    forward_entry = entering((summary_decay[0], summary_state[0]), "seq", combine, identity, False)
    reverse_entry = entering((summary_decay[1], summary_state[1]), "seq", combine, identity, True)
    entry_state = jnp.stack([forward_entry[1], reverse_entry[1]])
    span_entry = before_states + before_decay[..., None, None] * entry_state[None]
    span_entry = jnp.moveaxis(span_entry, 0, 1).astype(jnp.bfloat16)
    carried = jnp.einsum(
        "skin,skhpn->skihp", span_outputs, span_entry, preferred_element_type=jnp.float32
    )
    mixed = (
        intra_part
        + inflow[..., None] * carried
        + skip_gain[:, None] * span_values.astype(jnp.float32)
    )
    mixed = mixed.reshape(2, tok_count, heads_local * head_width)
    gate_wide = lax.optimization_barrier(gate_all).astype(jnp.float32)
    gated_out = mixed * jax.nn.silu(gate_wide)
    grouped = gated_out.reshape(2, tok_count, -1, GROUP_HEADS * head_width)
    normed = grouped * lax.rsqrt(jnp.mean(grouped * grouped, axis=3, keepdims=True) + 1e-05)
    normed = normed.reshape(2, tok_count, heads_local * head_width).astype(jnp.bfloat16)
    forward_mix = normed[0]
    reverse_mix = normed[1][::-1]
    block_cols = lax.all_gather(w_out, "seq", axis=1, tiled=True)
    direct = jnp.dot(forward_mix, block_cols, preferred_element_type=jnp.float32)
    flipped = jnp.dot(reverse_mix, block_cols, preferred_element_type=jnp.float32)[:, ::-1]
    running = direct
    running = running + flipped
    result = lax.psum_scatter(running, "mp", scatter_dimension=1, tiled=True).astype(jnp.bfloat16)
    return result[None]


def solution(mesh):
    placed = (
        P(("groups", "batch"), "seq", "mp"),
        P(("groups", "batch"), "seq"),
        P(),
        P("seq", "mp"),
        P("seq", "mp"),
        P("seq", "mp"),
        P("seq", "mp"),
        P("mp"),
        P("mp"),
        P("mp"),
        P(None, "mp"),
        P(None, "mp"),
        P("mp", "seq"),
    )
    return jax.shard_map(
        body,
        mesh=mesh,
        in_specs=placed,
        out_specs=P(("groups", "batch"), "seq", "mp"),
        check_vma=False,
    )
```

profile of v0, /device:TPU:0, one launch (start us, length us, event | category | flops | bytes accessed | tf_op | source)
XLA Modules:
  0.0 399.6 jit_solution(7486551002777506659)
XLA Ops:
  8.1 1.3 fusion.48
  9.3 5.4 %collective-permute-start.4 = (s32[1]{0:T(128)}, s32[1]{0:T(128)}, u32[]{:S(2)}, u32[]{:S(2)}) collective-permute-start(s32[1]{0:T(128)} %bitcast.30), channel_id=1, source_target_pairs={{0,4},{4,8},{8,12},{1,5},{5,9},{9,13},{2,6},{6,10},{10,14},{3,7},{... | collective-permute-start | bytes 20 | tf_op jit(solution)/shard_map/ppermute | solution.py:15
  14.7 1.3 collective-permute-start.5
  16.1 14.1 %all_gather.41 = bf16[2048,16]{0,1:T(8,128)(2,1)S(1)} all-gather(bf16[512,16]{0,1:T(8,128)(2,1)S(1)} %copy-done.17), channel_id=1, replica_groups=mesh['groups'=2,'seq'=4,'mp'=2,'batch'=2] {'seq'}, dimensions={0}, use_global_device_ids=true | all-gather | bytes 81920 | tf_op jit(solution)/shard_map/all_gather | solution.py:137
  30.5 17.5 %all_gather.39 = bf16[2048,128]{1,0:T(8,128)(2,1)} all-gather(bf16[512,128]{1,0:T(8,128)(2,1)S(1)} %copy-done.12), channel_id=1, replica_groups=mesh['groups'=2,'seq'=4,'mp'=2,'batch'=2] {'seq'}, dimensions={0}, use_global_device_ids=true | all-gather | bytes 655360 | tf_op jit(solution)/shard_map/all_gather | solution.py:136
  48.1 1.3 pad_add_fusion.1
  49.4 1.4 fusion.38
  50.8 12.6 %rev.13 = bf16[256,2048]{1,0:T(8,128)(2,1)S(1)} reverse(bf16[256,2048]{1,0:T(8,128)(2,1)} %bitcast.139), dimensions={0} | reverse | bytes 2097152 | tf_op jit(solution)/shard_map/rev | solution.py:128
  63.7 1.6 convert_multiply_fusion.1
  65.3 15.0 %rev.14 = f32[256,2048]{1,0:T(8,128)S(1)} reverse(f32[256,2048]{1,0:T(8,128)} %convert_multiply_fusion.1), dimensions={1} | reverse | bytes 4194304 | tf_op jit(solution)/shard_map/rev | solution.py:131
  83.5 1.2 reduce-window.6
  85.1 2.4 convolution_convert_fusion.2
  87.5 4.0 collective-permute-start.2
  91.5 1.3 collective-permute-start.3
  94.4 3.9 collective-permute-done.3
  98.5 16.9 %all-gather.10.cloned.1.call-done = bf16[2048,1024]{1,0:T(8,128)(2,1)} async-done(((bf16[512,1024]{1,0:T(8,128)(2,1)}), bf16[2048,1024]{1,0:T(8,128)(2,1)}) %all-gather.10.cloned.1.call-update) | async-done | bytes 4194320 | tf_op jit(solution)/shard_map/all_gather | solution.py:135
  115.4 4.5 %convolution_convert_fusion.1 = bf16[512,1024]{1,0:T(8,128)(2,1)S(1)} fusion(bf16[2048,1024]{1,0:T(8,128)(2,1)} %all-gather.10.cloned.1.call-done, bf16[256,2048]{1,0:T(8,128)(2,1)S(1)} %copy-done.9, bf16[256,2048]{1,0:T(8,128)(2,1)S(1)} %copy-done.7), kind=kOutput, calls=%fused_computation.44 | convolution fusion | flops 2152202240 | bytes 7340032 | tf_op jit(solution)/shard_map/dot_general | solution.py:140
  119.9 2.1 collective-permute-start
  122.0 1.3 collective-permute-start.1
  123.3 5.8 %all_gather.40 = bf16[2,256,256]{2,1,0:T(8,128)(2,1)S(1)} all-gather(bf16[2,256,128]{2,1,0:T(8,128)(2,1)S(1)} %multiply_convert_fusion.9), channel_id=1, replica_groups=mesh['groups'=2,'seq'=4,'mp'=2,'batch'=2] {'mp'}, dimensions={2}, use_global_device_ids=true | all-gather | bytes 393216 | tf_op jit(solution)/shard_map/all_gather | solution.py:154
  129.4 1.3 multiply_convert_fusion.4
  134.1 11.3 %all-gather.1 = bf16[4,1,16]{2,1,0:T(2,128)(2,1)S(1)} all-gather(bf16[1,1,16]{2,1,0:T(2,128)(2,1)S(1)} %get-tuple-element.338), channel_id=3, replica_groups=mesh['groups'=2,'seq'=4,'mp'=2,'batch'=2] {'seq'}, dimensions={0}, use_global_device_ids=true | all-gather | bytes 160 | tf_op jit(solution)/shard_map/all_gather | solution.py:32
  145.5 8.4 %all-gather.2 = bf16[4,1,16]{2,1,0:T(2,128)(2,1)S(1)} all-gather(bf16[1,1,16]{2,1,0:T(2,128)(2,1)S(1)} %get-tuple-element.339), channel_id=4, replica_groups=mesh['groups'=2,'seq'=4,'mp'=2,'batch'=2] {'seq'}, dimensions={0}, use_global_device_ids=true | all-gather | bytes 160 | tf_op jit(solution)/shard_map/all_gather | solution.py:32
  155.6 41.3 %all-gather.16.cloned.1.call-done = bf16[2048,1024]{1,0:T(8,128)(2,1)} async-done(((bf16[512,1024]{1,0:T(8,128)(2,1)}), bf16[2048,1024]{1,0:T(8,128)(2,1)}) %all-gather.16.cloned.1.call-update) | async-done | bytes 4194320 | tf_op jit(solution)/shard_map/all_gather | solution.py:134
  196.9 5.2 %convolution_convert_fusion = bf16[512,1024]{1,0:T(8,128)(2,1)S(1)} fusion(bf16[2048,1024]{1,0:T(8,128)(2,1)} %all-gather.16.cloned.1.call-done, bf16[256,2048]{1,0:T(8,128)(2,1)} %copy-done.8, bf16[256,2048]{1,0:T(8,128)(2,1)} %copy-done.6), kind=kOutput, calls=%fused_computation.43 | convolution fusion | flops 2152202240 | bytes 7340032 | tf_op jit(solution)/shard_map/dot_general | solution.py:140
  202.1 1.7 copy.94
  203.7 21.1 %all-gather.12.cloned.1.call-done = bf16[4,16,64,128]{3,2,1,0:T(8,128)(2,1)} async-done(((bf16[1,16,64,128]{3,2,1,0:T(8,128)(2,1)}), bf16[4,16,64,128]{3,2,1,0:T(8,128)(2,1)}) %all-gather.12.cloned.1.call-update) | async-done | bytes 1048592 | tf_op jit(solution)/shard_map/all_gather | solution.py:32
  224.8 4.5 %while.37 = (s32[]{:T(128)}, f32[16,64,128]{2,1,0:T(8,128)S(1)}, s32[]{:T(128)}, bf16[4,16]{1,0:T(4,128)(2,1)S(1)}, bf16[4,16,64,128]{3,2,1,0:T(8,128)(2,1)}, /*index=5*/s32[]{:T(128)}, s32[]{:T(128)}) while((s32[]{:T(128)}, f32[16,64,128]{2,1,0:T(8,128)S(1)}, s32[]{:T(128)}, bf16[4,16]{1,0:T(4,128)(2,1)S(1)}, ...), condition=%wide.region_5.6_spmd.clone, body=%wide.region_4.5_spmd.clone.sunk | while | flops 655380 | bytes 1310985 | solution.py:50
  225.9 1.1 fusion.60
  229.3 24.4 %all-gather.14.cloned.1.call-done = bf16[4,16,64,128]{3,2,1,0:T(8,128)(2,1)} async-done(((bf16[1,16,64,128]{3,2,1,0:T(8,128)(2,1)}), bf16[4,16,64,128]{3,2,1,0:T(8,128)(2,1)}) %all-gather.14.cloned.1.call-update) | async-done | bytes 1048592 | tf_op jit(solution)/shard_map/all_gather | solution.py:32
  253.7 4.5 %while.38 = (s32[]{:T(128)}, f32[16,64,128]{2,1,0:T(8,128)S(1)}, s32[]{:T(128)}, bf16[4,16]{1,0:T(4,128)(2,1)S(1)}, bf16[4,16,64,128]{3,2,1,0:T(8,128)(2,1)}, /*index=5*/s32[]{:T(128)}, s32[]{:T(128)}, s32[]{:T(128)}, s32[]{:T(128)}) while((s32[]{:T(128)}, f32[16,64,128]{2,1,0:T(8,128)S(1)}, s32[]{:T(128)}, ...), condition=%wide.region_7.8_spmd.clone, body=%wide.region_6.7_spmd.clone.sunk | while | flops 655384 | bytes 1311047 | solution.py:50
  254.8 1.1 fusion.61
  256.0 1.1 fusion.61
  257.1 1.1 fusion.61
  260.2 4.3 %fusion.20 = f32[2,1,256,16,64]{2,4,3,0,1:T(8,128)} fusion(f32[2,1,256,16,64]{2,4,3,0,1:T(8,128)S(1)} %bitcast.142, f32[2,256,16,64]{1,3,2,0:T(8,128)S(1)} %fusion.23, bf16[2,256,16,64]{1,3,2,0:T(8,128)(2,1)S(1)} %bitcast.147, f32[2,16,256]{2,1,0:T(8,128)S(1)} %copy-done.16, f32[2,16,256]{2,1,0:T(8,128)S(1)} %copy-done.13, ...), kind=kOutput, calls=%fused_computation.38 | convolution fusion | flops 283115520 | bytes 8093760 | tf_op jit(solution)/shard_map/vmap(vmap(hij,jhp->ihp))/dot_general | solution.py:64
  264.5 2.0 copy.95
  266.5 2.0 fusion.45
  268.4 4.1 %mul.393 = f32[2,256,2,512]{3,2,1,0:T(2,128)} reshape(f32[2,256,1024]{2,1,0:T(8,128)} %fusion.45) | data formatting | bytes 4194304 | tf_op jit(solution)/shard_map/mul | solution.py:199
  272.5 2.2 reduce_sum.29
  274.8 1.7 mul.394
  276.6 4.1 %mul.395 = f32[2,256,1024]{2,1,0:T(8,128)} reshape(f32[2,256,2,512]{3,2,1,0:T(2,128)} %mul.394) | data formatting | bytes 4194304 | tf_op jit(solution)/shard_map/mul | solution.py:199
  280.7 2.4 multiply_convert_fusion.2
  284.7 50.7 %all-gather.18.cloned.1.call-done = bf16[1024,2048]{1,0:T(8,128)(2,1)} async-done(((bf16[1024,512]{1,0:T(8,128)(2,1)}), bf16[1024,2048]{1,0:T(8,128)(2,1)}) %all-gather.18.cloned.1.call-update) | async-done | bytes 4194320 | tf_op jit(solution)/shard_map/all_gather | solution.py:203
  335.4 4.8 %fusion.49 = f32[256,2048]{1,0:T(8,128)} fusion(bf16[256,1024]{1,0:T(8,128)(2,1)S(1)} %rev.15, bf16[1024,2048]{1,0:T(8,128)(2,1)} %all-gather.18.cloned.1.call-done), kind=kOutput, calls=%fused_computation.125 | convolution fusion | flops 1073741824 | bytes 6815744 | tf_op jit(solution)/shard_map/dot_general | solution.py:205
  340.2 15.0 %rev.16 = f32[256,2048]{1,0:T(8,128)S(1)} reverse(f32[256,2048]{1,0:T(8,128)} %fusion.49), dimensions={1} | reverse | bytes 4194304 | tf_op jit(solution)/shard_map/rev | solution.py:205
  355.2 4.8 %convolution_add_fusion = f32[256,2048]{1,0:T(8,128)} fusion(f32[256,2048]{1,0:T(8,128)S(1)} %rev.16, bf16[1024,2048]{1,0:T(8,128)(2,1)} %all-gather.18.cloned.1.call-done, bf16[2,256,1024]{2,1,0:T(8,128)(2,1)S(1)} %copy-done.2), kind=kOutput, calls=%fused_computation.20 | convolution fusion | flops 1074266112 | bytes 8912896 | tf_op jit(solution)/shard_map/dot_general | solution.py:204
  360.1 30.5 %reduce-scatter.2.cloned.1.call-done = f32[256,1024]{1,0:T(8,128)} async-done(((f32[256,2048]{1,0:T(8,128)}), f32[256,1024]{1,0:T(8,128)}) %reduce-scatter.2.cloned.1.call-update) | async-done | bytes 1048592 | tf_op jit(solution)/shard_map/reduce_scatter | solution.py:208
  390.6 2.1 convert_bitcast_fusion
  (133 shorter events, 20.9 us)
Async XLA Ops:
  6.5 23.6 %copy-start.18 = (s32[1,256]{1,0:T(1,128)S(1)}, s32[1,256]{1,0:T(1,128)}, u32[]{:S(2)}) copy-start(s32[1,256]{1,0:T(1,128)} %param.18) | copy-start | bytes 3076
  6.5 9.6 %copy-start.17 = (bf16[512,16]{0,1:T(8,128)(2,1)S(1)}, bf16[512,16]{0,1:T(8,128)(2,1)}, u32[]{:S(2)}) copy-start(bf16[512,16]{0,1:T(8,128)(2,1)} %param.23) | copy-start | bytes 49156
  6.5 23.9 %copy-start.12 = (bf16[512,128]{1,0:T(8,128)(2,1)S(1)}, bf16[512,128]{1,0:T(8,128)(2,1)}, u32[]{:S(2)}) copy-start(bf16[512,128]{1,0:T(8,128)(2,1)} %param.22) | copy-start | bytes 393220
  6.5 41.5 %copy-start.20 = (bf16[4,128]{1,0:T(4,128)(2,1)S(1)}, bf16[4,128]{1,0:T(4,128)(2,1)}, u32[]{:S(2)}) copy-start(bf16[4,128]{1,0:T(4,128)(2,1)} %param.28) | copy-start | bytes 3076
  6.5 41.5 %copy-start.14 = (bf16[4,1024]{1,0:T(4,128)(2,1)S(1)}, bf16[4,1024]{1,0:T(4,128)(2,1)}, u32[]{:S(2)}) copy-start(bf16[4,1024]{1,0:T(4,128)(2,1)} %param.27) | copy-start | bytes 24580
  6.5 44.2 %all-gather.20.cloned.1.call-start = ((), (), s32[]{:S(2)}) async-start(), calls=%async_computation.7 | async-start | bytes 1572864 | tf_op jit(solution)/shard_map/all_gather | solution.py:127
  7.3 108.1 %all-gather.10.cloned.1.call-start = ((), (), s32[]{:S(2)}) async-start(), calls=%async_computation.1 | async-start | bytes 5242880 | tf_op jit(solution)/shard_map/all_gather | solution.py:135
  8.0 188.9 %all-gather.16.cloned.1.call-start = ((), (), s32[]{:S(2)}) async-start(), calls=%async_computation.4 | async-start | bytes 5242880 | tf_op jit(solution)/shard_map/all_gather | solution.py:134
  9.3 38.7 %collective-permute-start.4 = (s32[1]{0:T(128)}, s32[1]{0:T(128)}, u32[]{:S(2)}, u32[]{:S(2)}) collective-permute-start(s32[1]{0:T(128)} %bitcast.30), channel_id=1, source_target_pairs={{0,4},{4,8},{8,12},{1,5},{5,9},{9,13},{2,6},{6,10},{10,14},{3,7},{... | collective-permute-start | bytes 20 | tf_op jit(solution)/shard_map/ppermute | solution.py:15
  14.7 33.3 %collective-permute-start.5 = (s32[1]{0:T(128)}, s32[1]{0:T(128)}, u32[]{:S(2)}, u32[]{:S(2)}) collective-permute-start(s32[1]{0:T(128)} %bitcast.31), channel_id=1, source_target_pairs={{4,0},{8,4},{12,8},{5,1},{9,5},{13,9},{6,2},{10,6},{14,10},{7,3},{... | collective-permute-start | bytes 20 | tf_op jit(solution)/shard_map/ppermute | solution.py:18
  16.0 208.8 %all-gather.12.cloned.1.call-start = ((), (), s32[]{:S(2)}) async-start(), calls=%async_computation.2 | async-start | bytes 1310720 | tf_op jit(solution)/shard_map/all_gather | solution.py:32
  65.3 15.0 %copy-start = (bf16[1,256,2048]{2,1,0:T(8,128)(2,1)S(1)}, bf16[1,256,2048]{2,1,0:T(8,128)(2,1)}, u32[]{:S(2)}) copy-start(bf16[1,256,2048]{2,1,0:T(8,128)(2,1)} %all-gather.20.cloned.1.call-done) | copy-start | bytes 3145732
  65.3 15.3 %copy-start.19 = (f32[2048]{0:T(1024)S(1)}, f32[2048]{0:T(1024)}, u32[]{:S(2)}) copy-start(f32[2048]{0:T(1024)} %param.19) | copy-start | bytes 24580
  81.2 1.0 copy-start.6
  81.2 1.4 copy-start.8
  81.2 2.1 copy-start.21
  81.2 2.1 copy-start.22
  82.6 2.5 copy-start.10
  85.1 30.3 %copy-start.7 = (bf16[256,2048]{1,0:T(8,128)(2,1)S(1)}, bf16[256,2048]{1,0:T(8,128)(2,1)}, u32[]{:S(2)}) copy-start(bf16[256,2048]{1,0:T(8,128)(2,1)} %copy-done.6) | copy-start | bytes 3145732
  85.1 30.3 %copy-start.9 = (bf16[256,2048]{1,0:T(8,128)(2,1)S(1)}, bf16[256,2048]{1,0:T(8,128)(2,1)}, u32[]{:S(2)}) copy-start(bf16[256,2048]{1,0:T(8,128)(2,1)} %copy-done.8) | copy-start | bytes 3145732
  87.5 6.9 %collective-permute-start.2 = (bf16[3,128]{1,0:T(4,128)(2,1)S(1)}, bf16[3,128]{1,0:T(4,128)(2,1)S(1)}, u32[]{:S(2)}, u32[]{:S(2)}) collective-permute-start(bf16[3,128]{1,0:T(4,128)(2,1)S(1)} %get-tuple-element.318), channel_id=1, source_target_pairs={{0,4},{4,8},{8,12},{1,5},{5,9},{9,13},{2,6},{6,10},{10,14},{3,7},{... | collective-permute-start | bytes 2312 | tf_op jit(solution)/shard_map/ppermute | solution.py:26
  91.5 6.7 %collective-permute-start.3 = (bf16[3,128]{1,0:T(4,128)(2,1)S(1)}, bf16[3,128]{1,0:T(4,128)(2,1)S(1)}, u32[]{:S(2)}, u32[]{:S(2)}) collective-permute-start(bf16[3,128]{1,0:T(4,128)(2,1)S(1)} %get-tuple-element.319), channel_id=1, source_target_pairs={{4,0},{8,4},{12,8},{5,1},{9,5},{13,9},{6,2},{10,6},{14,10},{7,3},{... | collective-permute-start | bytes 2312 | tf_op jit(solution)/shard_map/ppermute | solution.py:26
  119.9 9.2 %collective-permute-start = (bf16[3,1024]{1,0:T(4,128)(2,1)S(1)}, bf16[3,1024]{1,0:T(4,128)(2,1)S(1)}, u32[]{:S(2)}, u32[]{:S(2)}) collective-permute-start(bf16[3,1024]{1,0:T(4,128)(2,1)S(1)} %get-tuple-element.314), channel_id=1, source_target_pairs={{0,4},{4,8},{8,12},{1,5},{5,9},{9,13},{2,6},{6,10},{10,14},{3,7},{... | collective-permute-start | bytes 18440 | tf_op jit(solution)/shard_map/ppermute | solution.py:26
  122.0 7.1 %collective-permute-start.1 = (bf16[3,1024]{1,0:T(4,128)(2,1)S(1)}, bf16[3,1024]{1,0:T(4,128)(2,1)S(1)}, u32[]{:S(2)}, u32[]{:S(2)}) collective-permute-start(bf16[3,1024]{1,0:T(4,128)(2,1)S(1)} %get-tuple-element.315), channel_id=1, source_target_pairs={{4,0},{8,4},{12,8},{5,1},{9,5},{13,9},{6,2},{10,6},{14,10},{7,3},{... | collective-permute-start | bytes 18440 | tf_op jit(solution)/shard_map/ppermute | solution.py:26
  131.2 2.5 copy-start.4
  132.6 121.1 %all-gather.14.cloned.1.call-start = ((), (), s32[]{:S(2)}) async-start(), calls=%async_computation.3 | async-start | bytes 1310720 | tf_op jit(solution)/shard_map/all_gather | solution.py:32
  133.1 202.3 %all-gather.18.cloned.1.call-start = ((), (), s32[]{:S(2)}) async-start(), calls=%async_computation.5 | async-start | bytes 5242880 | tf_op jit(solution)/shard_map/all_gather | solution.py:203
  133.7 256.9 %reduce-scatter.2.cloned.1.call-start = ((), (), s32[]{:S(2)}) async-start(), calls=%async_computation.6 | async-start | bytes 3145728 | tf_op jit(solution)/shard_map/reduce_scatter | solution.py:208
  258.2 1.6 copy-start.3
  258.2 1.8 copy-start.5
  258.2 2.0 copy-start.11
  258.3 2.0 copy-start.13
  258.3 2.0 copy-start.15
  258.3 1.9 copy-start.16
  258.3 1.9 copy-start.23
  283.1 1.0 copy-start.1
  340.2 15.0 %copy-start.2 = (bf16[2,256,1024]{2,1,0:T(8,128)(2,1)S(1)}, bf16[2,256,1024]{2,1,0:T(8,128)(2,1)}, u32[]{:S(2)}) copy-start(bf16[2,256,1024]{2,1,0:T(8,128)(2,1)} %copy-done.1) | copy-start | bytes 3145732
Sparse Core Ops, SparseCore 0:
  8.9 23.9 all-gather.19
  34.5 80.8 all-gather.9
  117.0 79.8 all-gather.15
  198.3 26.4 all-gather.11
  226.2 27.4 all-gather.13
  255.1 80.2 all-gather.17
  360.2 30.3 reduce-scatter.1
where the time goes:
time: 403 us; the launch traced here: 400 us
  waiting for transfers between devices  191 us (47%)
  local copies, waits for them, and re-layouts  64.4 us (16%)
  blocking collectives  57.2 us (14%)
  matrix products  28.5 us (7%)
  other arithmetic  28.4 us (7%)
  starting transfers between devices  15.6 us (4%)
  between operations  14 us (3%)
    all_gather x1, waiting for transfers between devices, body(): block_cols = lax.all_gather(w_out, 'seq', axis=1, tiled=True)  50.7 us
    all_gather x2, waiting for transfers between devices, entering(): lax.all_gather(part.astype(kind), axis)  45.4 us
    all_gather x1, waiting for transfers between devices, body(): lax.all_gather(w_gate, 'seq', axis=0, tiled=True)  41.3 us
    reduce_scatter x1, waiting for transfers between devices, body(): lax.psum_scatter(running, 'mp', scatter_dimension=1, tiled=True)  30.5 us
    all_gather x2, blocking collectives, entering(): lax.all_gather(part.astype(kind), axis)  19.8 us
    all_gather x1, blocking collectives, body(): lax.all_gather(w_in_out, 'seq', axis=0, tiled=True)  17.5 us
    all_gather x1, waiting for transfers between devices, body(): lax.all_gather(w_value, 'seq', axis=0, tiled=True)  16.9 us
    rev x1, local copies, waits for them, and re-layouts, body(): normalize(reverse_full)[:, ::-1] * norm_gain  15 us
  transfers between devices with their start and end apart: 13, of which 7 were waited for; matrix products, arithmetic and copies ran while one was open for 23% of the time, Pallas kernels for 0%

commit v1 on v0

--- a/solution.py
+++ b/solution.py
@@ -200,7 +200,12 @@
     normed = normed.reshape(2, tok_count, heads_local * head_width).astype(jnp.bfloat16)
     forward_mix = normed[0]
     reverse_mix = normed[1][::-1]
-    block_cols = lax.all_gather(w_out, "seq", axis=1, tiled=True)
+    ring = [w_out]
+    for hop in range(3):
+        ring.append(lax.ppermute(ring[-1], "seq", [(dev, (dev + 1) % 4) for dev in range(4)]))
+    block_cols = jnp.roll(
+        jnp.concatenate(ring[::-1], axis=1), (lax.axis_index("seq") + 1) * ring[0].shape[1], axis=1
+    )
     direct = jnp.dot(forward_mix, block_cols, preferred_element_type=jnp.float32)
     flipped = jnp.dot(reverse_mix, block_cols, preferred_element_type=jnp.float32)[:, ::-1]
     running = direct

time: 403 us -> 394 us (0.978)
  waiting for transfers between devices: 191 us -> 79.2 us
  blocking collectives: 57.2 us -> 118 us
  starting transfers between devices: 15.6 us -> 38 us
  local copies, waits for them, and re-layouts: 64.4 us -> 77.2 us
  other arithmetic: 28.4 us -> 32.7 us
    all_gather x1 -> x0, waiting for transfers between devices: 50.7 us -> none  [body(): block_cols = lax.all_gather(w_out, 'seq', axis=1, tiled=True)]
    all_gather x1, waiting for transfers between devices: 41.3 us -> 0.02 us  [body(): lax.all_gather(w_gate, 'seq', axis=0, tiled=True)]
    all_gather x2, blocking collectives: 19.8 us -> 58.8 us  [entering(): lax.all_gather(part.astype(kind), axis)]
    ppermute x0 -> x3, waiting for transfers between devices: none -> 23.9 us  [body(): lax.ppermute(ring[-1], 'seq', [(dev, (dev + 1) % 4) for dev in range(4)])]
    all_gather x2, waiting for transfers between devices: 45.4 us -> 22.4 us  [entering(): lax.all_gather(part.astype(kind), axis)]
    ppermute x0 -> x3, starting transfers between devices: none -> 22.7 us  [body(): lax.ppermute(ring[-1], 'seq', [(dev, (dev + 1) % 4) for dev in range(4)])]
    all_gather x1, blocking collectives: 14.1 us -> 31.7 us  [body(): lax.all_gather(w_step, 'seq', axis=0, tiled=True)]
    all_gather x1, waiting for transfers between devices: 16.9 us -> 0.02 us  [body(): lax.all_gather(w_value, 'seq', axis=0, tiled=True)]
  transfers between devices with their start and end apart: 13 -> 15, of which waited for: 7 -> 3; matrix products, arithmetic and copies ran while one was open for 23% -> 20% of each run, Pallas kernels for 0% -> 0%
where the time goes in v1:
time: 394 us; the launch traced here: 390 us
  blocking collectives  118 us (30%)
  waiting for transfers between devices  79.2 us (20%)
  local copies, waits for them, and re-layouts  77.2 us (20%)
  starting transfers between devices  38 us (10%)
  other arithmetic  32.7 us (8%)
  matrix products  30.9 us (8%)
  between operations  14.2 us (4%)
    all_gather x2, blocking collectives, entering(): lax.all_gather(part.astype(kind), axis)  58.8 us
    all_gather x1, blocking collectives, body(): lax.all_gather(w_step, 'seq', axis=0, tiled=True)  31.7 us
    reduce_scatter x1, waiting for transfers between devices, body(): lax.psum_scatter(running, 'mp', scatter_dimension=1, tiled=True)  31.4 us
    ppermute x3, waiting for transfers between devices, body(): lax.ppermute(ring[-1], 'seq', [(dev, (dev + 1) % 4) for dev in range(4)])  23.9 us
    ppermute x3, starting transfers between devices, body(): lax.ppermute(ring[-1], 'seq', [(dev, (dev + 1) % 4) for dev in range(4)])  22.7 us
    all_gather x2, waiting for transfers between devices, entering(): lax.all_gather(part.astype(kind), axis)  22.4 us
    all_gather x1, blocking collectives, body(): lax.all_gather(w_in_out, 'seq', axis=0, tiled=True)  21.9 us
    rev x1, local copies, waits for them, and re-layouts, body(): normalize(reverse_full)[:, ::-1] * norm_gain  17.8 us
  transfers between devices with their start and end apart: 15, of which 3 were waited for; matrix products, arithmetic and copies ran while one was open for 20% of the time, Pallas kernels for 0%

profile of v1, /device:TPU:0, one launch (start us, length us, event | category | flops | bytes accessed | tf_op | source)
XLA Modules:
  0.0 390.3 jit_solution(7247557841557117803)
XLA Ops:
  9.3 5.5 %collective-permute-start.4 = (s32[1]{0:T(128)}, s32[1]{0:T(128)}, u32[]{:S(2)}, u32[]{:S(2)}) collective-permute-start(s32[1]{0:T(128)} %bitcast.30), channel_id=1, source_target_pairs={{0,4},{4,8},{8,12},{1,5},{5,9},{9,13},{2,6},{6,10},{10,14},{3,7},{... | collective-permute-start | bytes 20 | tf_op jit(solution)/shard_map/ppermute | solution.py:15
  14.8 1.3 collective-permute-start.5
  16.1 2.7 collective-permute-start.6
  19.9 31.7 %all_gather.38 = bf16[2048,16]{0,1:T(8,128)(2,1)S(1)} all-gather(bf16[512,16]{0,1:T(8,128)(2,1)S(1)} %copy-done.24), channel_id=1, replica_groups=mesh['groups'=2,'seq'=4,'mp'=2,'batch'=2] {'seq'}, dimensions={0}, use_global_device_ids=true | all-gather | bytes 81920 | tf_op jit(solution)/shard_map/all_gather | solution.py:137
  51.6 21.9 %all_gather.36 = bf16[2048,128]{1,0:T(8,128)(2,1)} all-gather(bf16[512,128]{1,0:T(8,128)(2,1)S(1)} %copy-done.18), channel_id=1, replica_groups=mesh['groups'=2,'seq'=4,'mp'=2,'batch'=2] {'seq'}, dimensions={0}, use_global_device_ids=true | all-gather | bytes 655360 | tf_op jit(solution)/shard_map/all_gather | solution.py:136
  74.2 1.5 fusion.45
  75.7 1.4 pad_add_fusion.1
  77.2 12.6 %rev.13 = bf16[256,2048]{1,0:T(8,128)(2,1)S(1)} reverse(bf16[256,2048]{1,0:T(8,128)(2,1)} %bitcast.137), dimensions={0} | reverse | bytes 2097152 | tf_op jit(solution)/shard_map/rev | solution.py:128
  90.1 1.6 convert_multiply_fusion.1
  91.8 17.8 %rev.14 = f32[256,2048]{1,0:T(8,128)} reverse(f32[256,2048]{1,0:T(8,128)} %convert_multiply_fusion.1), dimensions={1} | reverse | bytes 4194304 | tf_op jit(solution)/shard_map/rev | solution.py:131
  109.8 2.2 fusion.18
  114.1 2.3 convolution_convert_fusion.2
  116.4 1.6 collective-permute-start.2
  117.9 1.3 collective-permute-start.3
  123.7 4.1 %collective-permute-start.7 = (bf16[1024,512]{1,0:T(8,128)(2,1)S(1)}, bf16[1024,512]{1,0:T(8,128)(2,1)}, u32[]{:S(2)}, u32[]{:S(2)}) collective-permute-start(bf16[1024,512]{1,0:T(8,128)(2,1)S(1)} %collective-permute-done.6), channel_id=1, source_target_pairs={{0,4},{4,8},{8,12},{12,0},{1,5},{5,9},{9,13},{13,1},{2,6},{6,10},{... | collective-permute-start | bytes 3145736 | tf_op jit(solution)/shard_map/ppermute | solution.py:205
  128.8 5.1 %convolution_convert_fusion.1 = bf16[512,1024]{1,0:T(8,128)(2,1)S(1)} fusion(bf16[2048,1024]{1,0:T(8,128)(2,1)} %all-gather.9.cloned.1.call-done, bf16[256,2048]{1,0:T(8,128)(2,1)} %copy-done.11, bf16[256,2048]{1,0:T(8,128)(2,1)S(1)} %copy-done.9), kind=kOutput, calls=%fused_computation.48 | convolution fusion | flops 2152202240 | bytes 7340032 | tf_op jit(solution)/shard_map/dot_general | solution.py:140
  133.9 4.0 %collective-permute-start = (bf16[3,1024]{1,0:T(4,128)(2,1)S(1)}, bf16[3,1024]{1,0:T(4,128)(2,1)S(1)}, u32[]{:S(2)}, u32[]{:S(2)}) collective-permute-start(bf16[3,1024]{1,0:T(4,128)(2,1)S(1)} %get-tuple-element.314), channel_id=1, source_target_pairs={{0,4},{4,8},{8,12},{1,5},{5,9},{9,13},{2,6},{6,10},{10,14},{3,7},{... | collective-permute-start | bytes 18440 | tf_op jit(solution)/shard_map/ppermute | solution.py:26
  137.9 1.3 collective-permute-start.1
  139.2 5.7 %all_gather.37 = bf16[2,256,256]{2,1,0:T(8,128)(2,1)S(1)} all-gather(bf16[2,256,128]{2,1,0:T(8,128)(2,1)S(1)} %multiply_convert_fusion.9), channel_id=1, replica_groups=mesh['groups'=2,'seq'=4,'mp'=2,'batch'=2] {'mp'}, dimensions={2}, use_global_device_ids=true | all-gather | bytes 393216 | tf_op jit(solution)/shard_map/all_gather | solution.py:154
  144.8 23.9 %collective-permute-done.7 = bf16[1024,512]{1,0:T(8,128)(2,1)} collective-permute-done((bf16[1024,512]{1,0:T(8,128)(2,1)S(1)}, bf16[1024,512]{1,0:T(8,128)(2,1)}, u32[]{:S(2)}, u32[]{:S(2)}) %collective-permute-start.7) | collective-permute-done | bytes 1048608 | tf_op jit(solution)/shard_map/ppermute | solution.py:205
  168.7 15.9 %collective-permute-start.8 = (bf16[1024,512]{1,0:T(8,128)(2,1)}, bf16[1024,512]{1,0:T(8,128)(2,1)}, u32[]{:S(2)}, u32[]{:S(2)}) collective-permute-start(bf16[1024,512]{1,0:T(8,128)(2,1)} %collective-permute-done.7), channel_id=1, source_target_pairs={{0,4},{4,8},{8,12},{12,0},{1,5},{5,9},{9,13},{13,1},{2,6},{6,10},{... | collective-permute-start | bytes 3145736 | tf_op jit(solution)/shard_map/ppermute | solution.py:205
  186.2 1.3 copy.85
  187.5 1.7 fusion.28
  190.1 50.6 %all-gather.1 = bf16[4,1,16]{2,1,0:T(2,128)(2,1)S(1)} all-gather(bf16[1,1,16]{2,1,0:T(2,128)(2,1)S(1)} %get-tuple-element.338), channel_id=3, replica_groups=mesh['groups'=2,'seq'=4,'mp'=2,'batch'=2] {'seq'}, dimensions={0}, use_global_device_ids=true | all-gather | bytes 160 | tf_op jit(solution)/shard_map/all_gather | solution.py:32
  240.8 8.1 %all-gather.2 = bf16[4,1,16]{2,1,0:T(2,128)(2,1)S(1)} all-gather(bf16[1,1,16]{2,1,0:T(2,128)(2,1)S(1)} %get-tuple-element.339), channel_id=4, replica_groups=mesh['groups'=2,'seq'=4,'mp'=2,'batch'=2] {'seq'}, dimensions={0}, use_global_device_ids=true | all-gather | bytes 160 | tf_op jit(solution)/shard_map/all_gather | solution.py:32
  250.1 1.4 constant_dynamic-update-slice_fusion.7
  251.4 1.5 constant_dynamic-update-slice_fusion.6
  253.2 1.4 constant_dynamic-update-slice_fusion.3
  254.6 1.4 constant_dynamic-update-slice_fusion.2
  256.4 3.3 copy-done.5
  259.9 5.8 %convolution_convert_fusion = bf16[512,1024]{1,0:T(8,128)(2,1)} fusion(bf16[2048,1024]{1,0:T(8,128)(2,1)} %all-gather.15.cloned.1.call-done, bf16[256,2048]{1,0:T(8,128)(2,1)} %copy-done.11, bf16[256,2048]{1,0:T(8,128)(2,1)S(1)} %copy-done.10), kind=kOutput, calls=%fused_computation.47 | convolution fusion | flops 2152202240 | bytes 7340032 | tf_op jit(solution)/shard_map/dot_general | solution.py:140
  265.8 1.6 copy.94
  267.4 4.5 %while.37 = (s32[]{:T(128)}, f32[16,64,128]{2,1,0:T(8,128)S(1)}, s32[]{:T(128)}, bf16[4,16]{1,0:T(4,128)(2,1)S(1)}, bf16[4,16,64,128]{3,2,1,0:T(8,128)(2,1)}, /*index=5*/s32[]{:T(128)}, s32[]{:T(128)}) while((s32[]{:T(128)}, f32[16,64,128]{2,1,0:T(8,128)S(1)}, s32[]{:T(128)}, bf16[4,16]{1,0:T(4,128)(2,1)S(1)}, ...), condition=%wide.region_5.6_spmd.clone, body=%wide.region_4.5_spmd.clone.sunk | while | flops 655380 | bytes 1310993 | solution.py:50
  271.9 22.4 %all-gather.13.cloned.1.call-done = bf16[4,16,64,128]{3,2,1,0:T(8,128)(2,1)} async-done(((bf16[1,16,64,128]{3,2,1,0:T(8,128)(2,1)}), bf16[4,16,64,128]{3,2,1,0:T(8,128)(2,1)}) %all-gather.13.cloned.1.call-update) | async-done | bytes 1048592 | tf_op jit(solution)/shard_map/all_gather | solution.py:32
  294.3 4.5 %while.38 = (s32[]{:T(128)}, f32[16,64,128]{2,1,0:T(8,128)S(1)}, s32[]{:T(128)}, bf16[4,16]{1,0:T(4,128)(2,1)S(1)}, bf16[4,16,64,128]{3,2,1,0:T(8,128)(2,1)}, /*index=5*/s32[]{:T(128)}, s32[]{:T(128)}, s32[]{:T(128)}, s32[]{:T(128)}) while((s32[]{:T(128)}, f32[16,64,128]{2,1,0:T(8,128)S(1)}, s32[]{:T(128)}, ...), condition=%wide.region_7.8_spmd.clone, body=%wide.region_6.7_spmd.clone.sunk | while | flops 655384 | bytes 1311055 | solution.py:50
  300.9 4.2 %fusion.27 = f32[2,1,256,16,64]{2,4,3,0,1:T(8,128)} fusion(f32[2,1,256,16,64]{2,4,3,0,1:T(8,128)S(1)} %bitcast.140, f32[2,256,16,64]{1,3,2,0:T(8,128)S(1)} %fusion.30, bf16[2,256,16,64]{1,3,2,0:T(8,128)(2,1)S(1)} %bitcast.145, f32[2,16,256]{2,1,0:T(8,128)S(1)} %copy-done.22, f32[2,16,256]{2,1,0:T(8,128)S(1)} %reduce_window_sum.30, ...), kind=kOutput, calls=%fused_computation.42 | convolution fusion | flops 283115520 | bytes 8093760 | tf_op jit(solution)/shard_map/vmap(vmap(hij,jhp->ihp))/dot_general | solution.py:64
  305.1 2.0 copy.95
  307.2 1.9 fusion.54
  309.1 4.0 %mul.396 = f32[2,256,2,512]{3,2,1,0:T(2,128)} reshape(f32[2,256,1024]{2,1,0:T(8,128)} %fusion.54) | data formatting | bytes 4194304 | tf_op jit(solution)/shard_map/mul | solution.py:199
  313.1 2.2 reduce_sum.29
  315.4 1.7 mul.397
  317.1 4.0 %mul.398 = f32[2,256,1024]{2,1,0:T(8,128)} reshape(f32[2,256,2,512]{3,2,1,0:T(2,128)} %mul.397) | data formatting | bytes 4194304 | tf_op jit(solution)/shard_map/mul | solution.py:199
  321.2 2.4 multiply_convert_fusion.2
  325.2 4.8 %fusion.9 = f32[256,2048]{1,0:T(8,128)} fusion(bf16[256,1024]{1,0:T(8,128)(2,1)S(1)} %rev.15, bf16[1024,4096]{1,0:T(8,128)(2,1)} %copy-done.5, s32[]{:T(128)S(6)} %select_n.98), kind=kOutput, calls=%fused_computation.14 | convolution fusion | flops 1073741824 | bytes 6815748 | tf_op jit(solution)/shard_map/dot_general | solution.py:210
  330.1 15.0 %rev.16 = f32[256,2048]{1,0:T(8,128)S(1)} reverse(f32[256,2048]{1,0:T(8,128)} %fusion.9), dimensions={1} | reverse | bytes 4194304 | tf_op jit(solution)/shard_map/rev | solution.py:210
  345.1 4.9 %fusion.13 = f32[256,2048]{1,0:T(8,128)} fusion(f32[256,2048]{1,0:T(8,128)S(1)} %rev.16, bf16[1024,4096]{1,0:T(8,128)(2,1)} %copy-done.5, s32[]{:T(128)S(6)} %select_n.98, bf16[2,256,1024]{2,1,0:T(8,128)(2,1)S(1)} %copy-done.4), kind=kOutput, calls=%fused_computation.24 | convolution fusion | flops 1074266112 | bytes 8912900 | tf_op jit(solution)/shard_map/dot_general | solution.py:209
  350.0 31.4 %reduce-scatter.2.cloned.1.call-done = f32[256,1024]{1,0:T(8,128)} async-done(((f32[256,2048]{1,0:T(8,128)}), f32[256,1024]{1,0:T(8,128)}) %reduce-scatter.2.cloned.1.call-update) | async-done | bytes 1048592 | tf_op jit(solution)/shard_map/reduce_scatter | solution.py:213
  381.3 2.1 convert_bitcast_fusion
  (162 shorter events, 29.6 us)
Async XLA Ops:
  6.5 12.4 %copy-start.25 = (s32[1,256]{1,0:T(1,128)S(1)}, s32[1,256]{1,0:T(1,128)}, u32[]{:S(2)}) copy-start(s32[1,256]{1,0:T(1,128)} %param.18) | copy-start | bytes 3076
  6.5 12.5 %copy-start.28 = (bf16[4,128]{1,0:T(4,128)(2,1)S(1)}, bf16[4,128]{1,0:T(4,128)(2,1)}, u32[]{:S(2)}) copy-start(bf16[4,128]{1,0:T(4,128)(2,1)} %param.28) | copy-start | bytes 3076
  6.5 13.3 %copy-start.20 = (bf16[4,1024]{1,0:T(4,128)(2,1)S(1)}, bf16[4,1024]{1,0:T(4,128)(2,1)}, u32[]{:S(2)}) copy-start(bf16[4,1024]{1,0:T(4,128)(2,1)} %param.27) | copy-start | bytes 24580
  6.5 13.3 %copy-start.24 = (bf16[512,16]{0,1:T(8,128)(2,1)S(1)}, bf16[512,16]{0,1:T(8,128)(2,1)}, u32[]{:S(2)}) copy-start(bf16[512,16]{0,1:T(8,128)(2,1)} %param.23) | copy-start | bytes 49156
  6.5 45.0 %copy-start.18 = (bf16[512,128]{1,0:T(8,128)(2,1)S(1)}, bf16[512,128]{1,0:T(8,128)(2,1)}, u32[]{:S(2)}) copy-start(bf16[512,128]{1,0:T(8,128)(2,1)} %param.22) | copy-start | bytes 393220
  6.5 70.7 %all-gather.17.cloned.1.call-start = ((), (), s32[]{:S(2)}) async-start(), calls=%async_computation.6 | async-start | bytes 1572864 | tf_op jit(solution)/shard_map/all_gather | solution.py:127
  7.3 121.5 %all-gather.9.cloned.1.call-start = ((), (), s32[]{:S(2)}) async-start(), calls=%async_computation.1 | async-start | bytes 5242880 | tf_op jit(solution)/shard_map/all_gather | solution.py:135
  8.0 251.9 %all-gather.15.cloned.1.call-start = ((), (), s32[]{:S(2)}) async-start(), calls=%async_computation.4 | async-start | bytes 5242880 | tf_op jit(solution)/shard_map/all_gather | solution.py:134
  9.3 64.9 %collective-permute-start.4 = (s32[1]{0:T(128)}, s32[1]{0:T(128)}, u32[]{:S(2)}, u32[]{:S(2)}) collective-permute-start(s32[1]{0:T(128)} %bitcast.30), channel_id=1, source_target_pairs={{0,4},{4,8},{8,12},{1,5},{5,9},{9,13},{2,6},{6,10},{10,14},{3,7},{... | collective-permute-start | bytes 20 | tf_op jit(solution)/shard_map/ppermute | solution.py:15
  14.8 59.4 %collective-permute-start.5 = (s32[1]{0:T(128)}, s32[1]{0:T(128)}, u32[]{:S(2)}, u32[]{:S(2)}) collective-permute-start(s32[1]{0:T(128)} %bitcast.31), channel_id=1, source_target_pairs={{4,0},{8,4},{12,8},{5,1},{9,5},{13,9},{6,2},{10,6},{14,10},{7,3},{... | collective-permute-start | bytes 20 | tf_op jit(solution)/shard_map/ppermute | solution.py:18
  16.1 107.7 %collective-permute-start.6 = (bf16[1024,512]{1,0:T(8,128)(2,1)}, bf16[1024,512]{1,0:T(8,128)(2,1)S(1)}, u32[]{:S(2)}, u32[]{:S(2)}) collective-permute-start(bf16[1024,512]{1,0:T(8,128)(2,1)} %param.29), channel_id=1, source_target_pairs={{0,4},{4,8},{8,12},{12,0},{1,5},{5,9},{9,13},{13,1},{2,6},{6,10},{... | collective-permute-start | bytes 3145736 | tf_op jit(solution)/shard_map/ppermute | solution.py:205
  18.8 248.6 %all-gather.11.cloned.1.call-start = ((), (), s32[]{:S(2)}) async-start(), calls=%async_computation.2 | async-start | bytes 1310720 | tf_op jit(solution)/shard_map/all_gather | solution.py:32
  91.8 17.8 %copy-start = (bf16[1,256,2048]{2,1,0:T(8,128)(2,1)S(1)}, bf16[1,256,2048]{2,1,0:T(8,128)(2,1)}, u32[]{:S(2)}) copy-start(bf16[1,256,2048]{2,1,0:T(8,128)(2,1)} %all-gather.17.cloned.1.call-done) | copy-start | bytes 3145732
  91.8 18.1 %copy-start.26 = (f32[2048]{0:T(1024)S(1)}, f32[2048]{0:T(1024)}, u32[]{:S(2)}) copy-start(f32[2048]{0:T(1024)} %param.19) | copy-start | bytes 24580
  112.0 1.0 copy-start.8
  112.0 1.3 copy-start.11
  112.0 2.0 copy-start.12
  114.1 5.2 %copy-start.29 = (f32[16]{0:T(128)S(1)}, f32[16]{0:T(128)}, u32[]{:S(2)}) copy-start(f32[16]{0:T(128)} %param.24) | copy-start | bytes 196
  114.1 5.2 %copy-start.31 = (f32[16]{0:T(128)S(1)}, f32[16]{0:T(128)}, u32[]{:S(2)}) copy-start(f32[16]{0:T(128)} %param.25) | copy-start | bytes 196
  116.3 12.4 %copy-start.9 = (bf16[256,2048]{1,0:T(8,128)(2,1)S(1)}, bf16[256,2048]{1,0:T(8,128)(2,1)}, u32[]{:S(2)}) copy-start(bf16[256,2048]{1,0:T(8,128)(2,1)} %copy-done.8) | copy-start | bytes 3145732
  116.4 11.5 %collective-permute-start.2 = (bf16[3,128]{1,0:T(4,128)(2,1)S(1)}, bf16[3,128]{1,0:T(4,128)(2,1)S(1)}, u32[]{:S(2)}, u32[]{:S(2)}) collective-permute-start(bf16[3,128]{1,0:T(4,128)(2,1)S(1)} %get-tuple-element.318), channel_id=1, source_target_pairs={{0,4},{4,8},{8,12},{1,5},{5,9},{9,13},{2,6},{6,10},{10,14},{3,7},{... | collective-permute-start | bytes 2312 | tf_op jit(solution)/shard_map/ppermute | solution.py:26
  117.9 9.9 %collective-permute-start.3 = (bf16[3,128]{1,0:T(4,128)(2,1)S(1)}, bf16[3,128]{1,0:T(4,128)(2,1)S(1)}, u32[]{:S(2)}, u32[]{:S(2)}) collective-permute-start(bf16[3,128]{1,0:T(4,128)(2,1)S(1)} %get-tuple-element.319), channel_id=1, source_target_pairs={{4,0},{8,4},{12,8},{5,1},{9,5},{13,9},{6,2},{10,6},{14,10},{7,3},{... | collective-permute-start | bytes 2312 | tf_op jit(solution)/shard_map/ppermute | solution.py:26
  120.6 13.3 %copy-start.14 = (f32[2,1,16,2,128]{4,2,3,1,0:T(8,128)}, f32[2,1,16,2,128]{4,2,3,1,0:T(8,128)S(1)}, u32[]{:S(2)}) copy-start(f32[2,1,16,2,128]{4,2,3,1,0:T(8,128)S(1)} %reduce-window.6) | copy-start | bytes 98308
  121.0 12.9 %copy-start.16 = (f32[2,16,2,128]{3,2,1,0:T(2,128)}, f32[2,16,2,128]{3,2,1,0:T(2,128)S(1)}, u32[]{:S(2)}) copy-start(f32[2,16,2,128]{3,2,1,0:T(2,128)S(1)} %broadcast.225) | copy-start | bytes 98308
  123.7 45.0 %collective-permute-start.7 = (bf16[1024,512]{1,0:T(8,128)(2,1)S(1)}, bf16[1024,512]{1,0:T(8,128)(2,1)}, u32[]{:S(2)}, u32[]{:S(2)}) collective-permute-start(bf16[1024,512]{1,0:T(8,128)(2,1)S(1)} %collective-permute-done.6), channel_id=1, source_target_pairs={{0,4},{4,8},{8,12},{12,0},{1,5},{5,9},{9,13},{13,1},{2,6},{6,10},{... | collective-permute-start | bytes 3145736 | tf_op jit(solution)/shard_map/ppermute | solution.py:205
  133.9 50.7 %collective-permute-start = (bf16[3,1024]{1,0:T(4,128)(2,1)S(1)}, bf16[3,1024]{1,0:T(4,128)(2,1)S(1)}, u32[]{:S(2)}, u32[]{:S(2)}) collective-permute-start(bf16[3,1024]{1,0:T(4,128)(2,1)S(1)} %get-tuple-element.314), channel_id=1, source_target_pairs={{0,4},{4,8},{8,12},{1,5},{5,9},{9,13},{2,6},{6,10},{10,14},{3,7},{... | collective-permute-start | bytes 18440 | tf_op jit(solution)/shard_map/ppermute | solution.py:26
  137.9 46.7 %collective-permute-start.1 = (bf16[3,1024]{1,0:T(4,128)(2,1)S(1)}, bf16[3,1024]{1,0:T(4,128)(2,1)S(1)}, u32[]{:S(2)}, u32[]{:S(2)}) collective-permute-start(bf16[3,1024]{1,0:T(4,128)(2,1)S(1)} %get-tuple-element.315), channel_id=1, source_target_pairs={{4,0},{8,4},{12,8},{5,1},{9,5},{13,9},{6,2},{10,6},{14,10},{7,3},{... | collective-permute-start | bytes 18440 | tf_op jit(solution)/shard_map/ppermute | solution.py:26
  168.7 81.4 %collective-permute-start.8 = (bf16[1024,512]{1,0:T(8,128)(2,1)}, bf16[1024,512]{1,0:T(8,128)(2,1)}, u32[]{:S(2)}, u32[]{:S(2)}) collective-permute-start(bf16[1024,512]{1,0:T(8,128)(2,1)} %collective-permute-done.7), channel_id=1, source_target_pairs={{0,4},{4,8},{8,12},{12,0},{1,5},{5,9},{9,13},{13,1},{2,6},{6,10},{... | collective-permute-start | bytes 3145736 | tf_op jit(solution)/shard_map/ppermute | solution.py:205
  186.2 1.4 copy-start.23
  186.2 1.3 copy-start.30
  187.5 2.6 copy-start.27
  187.5 61.4 %copy-start.17 = (f32[2,16,2,128]{3,2,1,0:T(2,128)S(1)}, f32[2,16,2,128]{3,2,1,0:T(2,128)}, u32[]{:S(2)}) copy-start(f32[2,16,2,128]{3,2,1,0:T(2,128)} %copy-done.16) | copy-start | bytes 98308
  187.5 61.4 %copy-start.15 = (f32[2,1,16,2,128]{4,2,3,1,0:T(8,128)S(1)}, f32[2,1,16,2,128]{4,2,3,1,0:T(8,128)}, u32[]{:S(2)}) copy-start(f32[2,1,16,2,128]{4,2,3,1,0:T(8,128)} %copy-done.14) | copy-start | bytes 98308
  190.1 104.3 %all-gather.13.cloned.1.call-start = ((), (), s32[]{:S(2)}) async-start(), calls=%async_computation.3 | async-start | bytes 1310720 | tf_op jit(solution)/shard_map/all_gather | solution.py:32
  251.4 1.6 copy-start.1
  256.2 3.7 copy-start.10
  256.3 3.3 copy-start.5
  259.7 121.7 %reduce-scatter.2.cloned.1.call-start = ((), (), s32[]{:S(2)}) async-start(), calls=%async_computation.5 | async-start | bytes 3145728 | tf_op jit(solution)/shard_map/reduce_scatter | solution.py:213
  298.9 1.6 copy-start.6
  298.9 1.8 copy-start.7
  298.9 2.0 copy-start.13
  298.9 2.0 copy-start.19
  298.9 2.0 copy-start.21
  298.9 2.0 copy-start.22
  298.9 2.0 copy-start.32
  305.1 2.0 copy-start.2
  323.5 1.0 copy-start.3
  330.1 15.0 %copy-start.4 = (bf16[2,256,1024]{2,1,0:T(8,128)(2,1)S(1)}, bf16[2,256,1024]{2,1,0:T(8,128)(2,1)}, u32[]{:S(2)}) copy-start(bf16[2,256,1024]{2,1,0:T(8,128)(2,1)} %copy-done.3) | copy-start | bytes 3145732
Sparse Core Ops, SparseCore 0:
  8.9 23.9 all-gather.16
  34.5 89.5 all-gather.8
  125.7 112.1 all-gather.14
  239.3 26.1 all-gather.10
  266.9 27.4 all-gather.12
  350.1 31.1 reduce-scatter.1
